TPU v7x, 32 devices: a whole 2x2x4 slice. The times are simulated.
32 devices in a mesh: groups: 2 (over x), row: 4 (over y, core), col: 4 (over z).
Axes of the slice: x: 2, y: 2, z: 4, core: 2. Of those that a mesh axis runs over, the one named last changes fastest.
Arguments:
- positions: float32 [3, 32768], P(None, ('groups', 'row', 'col')), parts along dimension 1, may hold values from -6 to 6
- strengths: float32 [3, 32768], P(None, ('groups', 'row', 'col')), parts along dimension 1, may hold values from -6 to 6
- cores: float32 [32768], P(('groups', 'row', 'col')), parts along dimension 0, may hold values from 0.3 to 1
- order: int32 [32768], P(('groups', 'row', 'col')), parts along dimension 0, may hold values from 0 to 1023, as said below
- tile_counts: int32 [256], P(('groups', 'row', 'col')), parts along dimension 0, may hold values from 32 to 128
- pair_slots: int32 [2, 2048], P(None, ('groups', 'row', 'col')), parts along dimension 1, may hold values from 0 to 31, as said below
- pair_count: int32 [32], P(('groups', 'row', 'col')), parts along dimension 0, may hold values from 16 to 64, as said below
Outputs:
- velocity: float32 [3, 32768], P(None, ('groups', 'row', 'col')), parts along dimension 1
- stretching: float32 [3, 32768], P(None, ('groups', 'row', 'col')), parts along dimension 1
There are 2 independent parts, one for each index of `groups`. A program takes and returns all parts, laid end to end along the dimension named above; each array names one. Nothing has to cross between parts.
Inputs may be any that keep to these rules, and one draw needn't show every extreme that they name: `order`: each device's block of 1024 entries is a permutation of 0 to 1023. `pair_slots`: row 0 is below 32, row 1 below 32; the first 8 slots of every device pair each of its own tiles with itself. `pair_count`: some device has all its slots live.
All inputs are finite; a program needn't handle non-finite values.
Results may differ from a plain program's by a relative error of at most 0.0001.
Values sent between devices are 32-bit elements; how exact they have to be, the bound alone decides.
No kernel may reach another device: no remote copies, remote signals or barrier semaphores. Data moves between devices by JAX's collectives and lax.ppermute only.
A program may use at most 64 MiB of HBM per device.

v0:
```python
import functools
import math

import jax
import jax.numpy as jnp
from jax import lax
from jax.experimental import pallas as pl
from jax.experimental.pallas import tpu as pltpu
from jax.sharding import PartitionSpec as P

TILE = 128
ROWS = 8
STEPS = 4
LEAD = 2
FEAT = 32
TERMS = 64
VMEM_BYTES = 48 * 1024 * 1024

biot_factor = -1.0 / (4.0 * math.pi)


def row_ids(count=ROWS):
    return lax.broadcasted_iota(jnp.int32, (count, TILE), 0)


def roll_rows(value, shift):
    return pltpu.roll(value, shift % ROWS, 0)


def pack_kernel(
    counts_hbm, pos_hbm, str_hbm, core_hbm, order_hbm, slots_hbm,
    out_ref, slots_ref, stored, order_ref, counts_ref, arrived,
):
    tiles = order_ref.shape[1] // TILE
    pairs = (
        (pos_hbm, stored.at[0:3, :]),
        (str_hbm, stored.at[3:6, :]),
        (core_hbm, stored.at[6:7, :]),
        (order_hbm, order_ref),
        (counts_hbm, counts_ref),
        (slots_hbm, slots_ref),
    )
    copies = [pltpu.make_async_copy(src, dst, arrived.at[k]) for k, (src, dst) in enumerate(pairs)]
    for copy in copies:
        copy.start()
    stored[7:8, :] = jnp.zeros((1, stored.shape[1]), jnp.float32)
    for copy in copies:
        copy.wait()
    lane = lax.broadcasted_iota(jnp.int32, (ROWS, TILE), 1)
    rows = row_ids()
    is_strength = (rows >= 3) & (rows < 6)
    for tile in range(tiles):
        where_from = jnp.broadcast_to(order_ref[:, tile * TILE : (tile + 1) * TILE], (ROWS, TILE))
        inside = where_from & (TILE - 1)
        block = where_from >> 7
        value = jnp.zeros((ROWS, TILE), jnp.float32)
        for source in range(tiles):
            part = jnp.take_along_axis(stored[:, source * TILE : (source + 1) * TILE], inside, axis=1)
            value = jnp.where(block == source, part, value)
        live = lane < counts_ref[tile]
        value = jnp.where(is_strength & ~live, 0.0, value)
        value = jnp.where(rows == 7, live.astype(jnp.float32), value)
        out_ref[tile * ROWS : (tile + 1) * ROWS, :] = value


def split_three(value):
    first = value.astype(jnp.bfloat16).astype(jnp.float32)
    rest = value - first
    second = rest.astype(jnp.bfloat16).astype(jnp.float32)
    return first, second, rest - second


def split_two(value):
    high = value.astype(jnp.bfloat16)
    return high, (value - high.astype(jnp.float32)).astype(jnp.bfloat16)


def add_pieces(terms):
    return terms[0:ROWS, :] + (terms[ROWS : 2 * ROWS, :] + terms[2 * ROWS : 3 * ROWS, :])


def cross(left, right):
    return [left[1] * right[2] - left[2] * right[1], left[2] * right[0] - left[0] * right[2], left[0] * right[1] - left[1] * right[0]]


def describe(tile_row, origin):
    position = [tile_row(k) - origin[k : k + 1, :] for k in range(3)]
    strength = [tile_row(3 + k) for k in range(3)]
    core = tile_row(6)
    half = 0.5 * core * core
    coarse = [value.astype(jnp.bfloat16).astype(jnp.float32) for value in position]
    norm = coarse[0] * coarse[0] + coarse[1] * coarse[1] + coarse[2] * coarse[2]
    rest = [(value - near) * (value + near) for value, near in zip(position, coarse)]
    rest = rest[0] + rest[1] + rest[2] + half
    along = position[0] * strength[0] + position[1] * strength[1] + position[2] * strength[2]
    return position, strength, half, norm, rest, along


def put_rows(ref, start, tiles, values):
    for row, value in values.items():
        ref[pl.ds(start + row, tiles, stride=ROWS), :] = value


def negative(values):
    return [-value for value in values]


def numbered(first, values):
    return dict(enumerate(values, first))


def stage_features(ref, start, tiles, position, strength):
    put_rows(ref, start, tiles, numbered(0, strength + cross(position, strength)))


def stage_target(refs, start, tiles, description):
    position, strength, half, norm, rest, along = description
    put_rows(refs[0], start, tiles, numbered(0, position + strength))
    put_rows(refs[1], start, tiles, numbered(0, [norm, rest, along, half]))


def stage_source(refs, start, tiles, description):
    position, strength, half, norm, rest, along = description
    put_rows(refs[0], start, tiles, numbered(0, [-2.0 * value for value in position]) | {6: norm, 7: rest})
    put_rows(refs[1], start, tiles, numbered(3, negative(position)))
    put_rows(refs[2], start, tiles, numbered(0, negative(strength)) | {6: along})
    put_rows(refs[3], start, tiles, {6: half})


def features(tile, rows):
    value = jnp.where(rows < 6, tile, 0.0)
    return jnp.concatenate([*split_three(value), jnp.zeros_like(value)], axis=0).astype(jnp.bfloat16)


def target_side(shared, alone, rows):
    first, second, third = split_three(jnp.where(rows < 6, shared, 1.0))
    alone1, alone2, alone3 = split_three(jnp.where(rows < 4, alone, 0.0))
    both = jnp.where(rows < 4, alone1, roll_rows(alone2, 4))
    stacked = jnp.concatenate([first, both, first, first, second, second, third, alone3], axis=0)
    return stacked.astype(jnp.bfloat16).T


def source_side(dist, front, back, core, rows):
    zero = jnp.zeros_like(dist)
    one = jnp.ones_like(dist)
    values = (
        jnp.where((rows < 3) | (rows > 5), dist, 0.0),
        jnp.where((rows >= 3) & (rows < 6), front, 0.0),
        jnp.where((rows < 3) | (rows == 6), back, 0.0),
        jnp.where(rows == 6, core, 0.0),
    )
    pick = rows & 3
    picks = (jnp.where(pick < 2, one, zero), jnp.where(pick == 2, one, zero), zero, jnp.where(pick == 3, one, zero))
    blocks = []
    for value, picked in zip(values, picks):
        first, second, third = split_three(value)
        parts = [first, picked, second, third, first, second, first, picked]
        blocks.append(jnp.concatenate(parts, axis=0).astype(jnp.bfloat16))
    return jnp.concatenate(blocks, axis=1)


def finish_block(tile_row, smooth_row, grad_row, origin):
    position = [tile_row(k) - origin[k : k + 1, :] for k in range(3)]
    strength = [tile_row(3 + k) for k in range(3)]
    scale = biot_factor * tile_row(7)
    smooth = [smooth_row(k) for k in range(6)]
    grad = [grad_row(k) for k in range(6)]
    velocity = [turn - part for turn, part in zip(cross(position, smooth[:3]), smooth[3:])]
    lever = [turn - part for turn, part in zip(cross(position, grad[:3]), grad[3:])]
    stretch = [turn - 3.0 * part for turn, part in zip(cross(strength, smooth[:3]), lever)]
    return [scale * value for value in velocity + stretch]


def evaluate(products, pieces):
    for start in range(0, TILE, 16):
        at = slice(start, start + 16)
        dist, front, back, core = (products[at, k * TILE : (k + 1) * TILE] for k in range(4))
        inv = lax.rsqrt(dist)
        inv2 = inv * inv
        inv3 = inv2 * inv
        tail = core * (inv3 * inv2)
        smooth = inv3 + 1.5 * tail
        grad = inv2 * (smooth + tail)
        for k, value in enumerate((smooth, grad * front, grad * back)):
            high, low = split_two(value)
            pieces[at, 2 * k * TILE : (2 * k + 1) * TILE] = high
            pieces[at, (2 * k + 1) * TILE : (2 * k + 2) * TILE] = low


def tile_at(tile):
    return pl.ds(pl.multiple_of(tile * ROWS, ROWS), ROWS)


def term_at(tile):
    return pl.ds(pl.multiple_of(tile * TERMS, TERMS), TERMS)


def wide_at(tile):
    return pl.ds(pl.multiple_of(tile * TILE, TILE), TILE)


def feat_at(tile):
    return pl.ds(pl.multiple_of(tile * FEAT, FEAT), FEAT)


def target_terms(feat, values):
    smooth, front = values[:, : 2 * TILE], values[:, 2 * TILE : 4 * TILE]
    terms = lax.dot_general(
        jnp.concatenate([feat, feat], axis=1),
        jnp.concatenate([smooth, front], axis=0),
        (((1,), (1,)), ((), ())),
        preferred_element_type=jnp.float32,
    )
    return add_pieces(terms)


def source_terms(feat, values):
    high = jnp.concatenate([values[:, :TILE], values[:, 4 * TILE : 5 * TILE]], axis=1)
    low = jnp.concatenate([values[:, TILE : 2 * TILE], values[:, 5 * TILE :]], axis=1)
    both = jnp.concatenate([high, low], axis=0)
    terms = jnp.dot(jnp.concatenate([feat, feat], axis=1), both, preferred_element_type=jnp.float32)
    return add_pieces(terms)


def own_kernel(block, left, right, feat, sums, origin_ref, *scratch):
    products, pieces = scratch[:STEPS], scratch[STEPS : 2 * STEPS]
    stages, copied = scratch[2 * STEPS : -1], scratch[-1]
    copied[: block.shape[0], :] = block[...]
    tiles = block.shape[0] // ROWS
    rows = row_ids()
    total = block[0:ROWS, :]
    for tile in range(1, tiles):
        total = total + block[tile * ROWS : (tile + 1) * ROWS, :]
    origin = jnp.sum(total, axis=1, keepdims=True) * (1.0 / (tiles * TILE))
    origin = jnp.where(rows < 3, jnp.broadcast_to(origin, (ROWS, TILE)), 0.0)
    origin_ref[...] = origin
    description = describe(lambda row: copied[pl.ds(row, tiles, stride=ROWS), :], origin)
    stage_features(stages[0], 0, tiles, *description[:2])
    stage_target(stages[1:3], 0, tiles, description)
    stage_source(stages[3:], 0, tiles, description)
    for tile in range(tiles):
        staged = [ref[tile * ROWS : (tile + 1) * ROWS, :] for ref in stages]
        feat[tile * FEAT : (tile + 1) * FEAT, :] = features(staged[0], rows)
        left[tile * TILE : (tile + 1) * TILE, :] = target_side(*staged[1:3], rows)
        right[tile * TERMS : (tile + 1) * TERMS, :] = source_side(*staged[3:], rows)
    for step in range(tiles + 2 * LEAD):
        if step < tiles:
            target, source = left[step * TILE : (step + 1) * TILE, :], right[step * TERMS : (step + 1) * TERMS, :]
            products[step % STEPS][...] = jnp.dot(target, source, preferred_element_type=jnp.float32)
        if LEAD <= step < tiles + LEAD:
            evaluate(products[(step - LEAD) % STEPS], pieces[(step - LEAD) % STEPS])
        if step >= 2 * LEAD:
            tile = step - 2 * LEAD
            terms = target_terms(feat[tile * FEAT : (tile + 1) * FEAT, :], pieces[tile % STEPS])
            sums[tile * ROWS : (tile + 1) * ROWS, :] = terms


def join_kernel(*refs):
    out, start = refs[-1], 0
    for ref in refs[:-1]:
        out[start : start + ref.shape[0], :] = ref[...]
        start += ref.shape[0]


def pair_kernel(nrows, ncols, tiles, where_ref, slots_ref, *refs):
    own_block, own_left, own_right, own_feat, own_sums, origin_ref = refs[:6]
    refs = refs[6:]
    halves = nrows // 2
    row_ins, far_ins, near_in, refs = refs[: ncols - 1], refs[ncols - 1 : ncols + halves - 2], refs[ncols + halves - 2], refs[ncols + halves - 1 :]
    row_outs, col_outs, scratch = refs[:ncols], refs[ncols : ncols + halves], refs[ncols + halves :]
    left, right, row_feat, col_feat = scratch[:4]
    row_sum, col_sum = scratch[4:6], scratch[6:8]
    row_stage, col_stage = scratch[8:11], scratch[11:16]
    came, done = scratch[16:18]
    products, pieces = scratch[18 : 18 + STEPS], scratch[18 + STEPS :]
    per = tiles * ROWS
    rows = row_ids()
    my_row, my_col = where_ref[0], where_ref[1]
    count = where_ref[2]
    for number, ref in enumerate((own_block, *row_ins, *far_ins)):
        came[number * per : (number + 1) * per, :] = ref[...]
    near = ncols + halves - 1
    came[near * per : (near + halves) * per, :] = near_in[...]
    row_sources = [(k, k * per) for k in range(1, ncols)]
    col_sources = [(2 * m, (ncols - 1 + m) * per) for m in range(1, halves)]
    col_sources += [(2 * m + 1, (near + m) * per) for m in range(halves)]
    origin = origin_ref[...]

    for ref in (*row_sum, *col_sum):
        ref[...] = jnp.zeros_like(ref)
    for k in range(STEPS - LEAD, STEPS):
        pieces[k][...] = jnp.zeros_like(pieces[k])
    for feat, me in ((row_feat, my_col), (col_feat, my_row)):
        feat[pl.ds(pl.multiple_of(me * tiles * FEAT, tiles * FEAT), tiles * FEAT), :] = own_feat[...]
    for k, ref in enumerate(row_sum):
        ref[pl.ds(pl.multiple_of(my_col * per, per), per), :] = own_sums[:, k * TILE : (k + 1) * TILE]
    left[pl.ds(pl.multiple_of(my_col * tiles * TILE, tiles * TILE), tiles * TILE), :] = own_left[...]
    right[pl.ds(pl.multiple_of(my_row * tiles * TERMS, tiles * TERMS), tiles * TERMS), :] = own_right[...]

    def rows_of(ref, start):
        return lambda row: ref[pl.ds(start + row, tiles, stride=ROWS), :]

    for number, (_, start) in enumerate(row_sources):
        description = describe(rows_of(came, start), origin)
        stage_features(row_stage[0], number * per, tiles, *description[:2])
        stage_target(row_stage[1:], number * per, tiles, description)
    for number, (_, start) in enumerate(col_sources):
        description = describe(rows_of(came, start), origin)
        stage_features(col_stage[0], number * per, tiles, *description[:2])
        stage_source(col_stage[1:], number * per, tiles, description)

    def prepare(step, carry):
        for number, (k, _) in enumerate(row_sources):
            tile = (my_col ^ k) * tiles + step
            staged = [ref[pl.ds(pl.multiple_of(number * per + step * ROWS, ROWS), ROWS), :] for ref in row_stage]
            row_feat[feat_at(tile), :] = features(staged[0], rows)
            left[wide_at(tile), :] = target_side(*staged[1:], rows)
        for number, (k, _) in enumerate(col_sources):
            tile = (my_row ^ k) * tiles + step
            staged = [ref[pl.ds(pl.multiple_of(number * per + step * ROWS, ROWS), ROWS), :] for ref in col_stage]
            col_feat[feat_at(tile), :] = features(staged[0], rows)
            right[term_at(tile), :] = source_side(*staged[1:], rows)
        return carry

    lax.fori_loop(0, tiles, prepare, 0, unroll=2)

    last = slots_ref.shape[1] - 1

    def multiply(slot, out):
        slot = jnp.minimum(slot, last)
        tgt, src = slots_ref[0, slot], slots_ref[1, slot]
        out[...] = jnp.dot(left[wide_at(tgt), :], right[term_at(src), :], preferred_element_type=jnp.float32)

    def add_up(slot, values):
        kept = jnp.clip(slot, 0, last)
        tgt, src = slots_ref[0, kept], slots_ref[1, kept]
        own = (tgt // tiles == my_col) & (src // tiles == my_row) & (tgt % tiles == src % tiles)
        alive = jnp.where((slot >= tiles) & (slot < count), 1.0, 0.0)
        react = jnp.where(own, 0.0, alive)
        to_target = alive * target_terms(col_feat[feat_at(src), :], values)
        to_source = react * source_terms(row_feat[feat_at(tgt), :], values)
        for k in range(2):
            row_sum[k][tile_at(tgt), :] += to_target[:, k * TILE : (k + 1) * TILE]
            col_sum[k][tile_at(src), :] += to_source[:, k * TILE : (k + 1) * TILE]

    for k in range(LEAD):
        multiply(tiles + k, products[k])
    loops = (count - tiles + STEPS - 1) // STEPS

    def visit(step, carry):
        for k in range(STEPS):
            slot = tiles + step * STEPS + k
            multiply(slot + LEAD, products[(k + LEAD) % STEPS])
            evaluate(products[k], pieces[k])
            add_up(slot - LEAD, pieces[(k - LEAD) % STEPS])
        return carry

    lax.fori_loop(0, loops, visit, 0)
    for k in range(LEAD):
        add_up(tiles + loops * STEPS - LEAD + k, pieces[STEPS - LEAD + k])

    row_results = [(k, row_outs[k], 0) for k in range(ncols)]
    col_results = [(k, col_outs[k // 2], k % 2 * per) for k in range(nrows)]
    number = 0
    for results, sources, sums, me in (
        (row_results, row_sources, row_sum, my_col),
        (col_results, col_sources, col_sum, my_row),
    ):
        starts = dict(sources) | {0: 0}
        for k, result, start in results:
            base = pl.multiple_of((me ^ k) * per, per)
            values = finish_block(rows_of(came, starts[k]), *(rows_of(ref, base) for ref in sums), origin)
            put_rows(done, number * per, tiles, numbered(0, values))
            result[start : start + per, :] = done[number * per : (number + 1) * per, :]
            number += 1


def halve_kernel(*refs):
    keep, send = refs[-2:]
    half = keep.shape[0]
    total = refs[0][...]
    for ref in refs[1:-2]:
        total = total + ref[...]
    keep[...] = total[:half, :]
    send[...] = total[half:, :]


def total_kernel(*refs):
    vel_ref, str_ref = refs[-2:]
    tiles = vel_ref.shape[1] // TILE
    for tile in range(tiles):
        at = slice(tile * ROWS, (tile + 1) * ROWS)
        total = refs[0][at, :]
        for ref in refs[1:-2]:
            total = total + ref[at, :]
        vel_ref[:, tile * TILE : (tile + 1) * TILE] = total[0:3, :]
        str_ref[:, tile * TILE : (tile + 1) * TILE] = total[3:6, :]


def shards(positions, strengths, cores, order, tile_counts, pair_slots, pair_count):
    tiles = tile_counts.shape[0]
    per_dev = tiles * TILE
    nrows = lax.axis_size("row")
    ncols = lax.axis_size("col")
    halves = nrows // 2
    assert nrows == 2 * halves and nrows & (nrows - 1) == 0 and ncols & (ncols - 1) == 0
    row_tiles, col_tiles = ncols * tiles, nrows * tiles
    smem = pl.BlockSpec(memory_space=pltpu.SMEM)
    vmem = pl.BlockSpec(memory_space=pltpu.VMEM)
    hbm = pl.BlockSpec(memory_space=pltpu.HBM)
    params = pltpu.CompilerParams(vmem_limit_bytes=VMEM_BYTES)

    def blocks(count):
        return jax.ShapeDtypeStruct((count * tiles * ROWS, TILE), jnp.float32)

    def in_hbm(value):
        return pltpu.with_memory_space_constraint(value, pltpu.HBM)

    inputs = (tile_counts, positions, strengths, cores.reshape(1, per_dev), order.reshape(1, per_dev), pair_slots)
    packed, slots = pl.pallas_call(
        pack_kernel,
        out_shape=[blocks(1), jax.ShapeDtypeStruct(pair_slots.shape, jnp.int32)],
        in_specs=[hbm] * len(inputs),
        out_specs=[vmem, smem],
        scratch_shapes=[
            pltpu.VMEM((ROWS, per_dev), jnp.float32),
            pltpu.VMEM((1, per_dev), jnp.int32),
            pltpu.SMEM(tile_counts.shape, jnp.int32),
            pltpu.SemaphoreType.DMA((len(inputs),)),
        ],
        compiler_params=params,
        name="pack",
    )(*map(in_hbm, inputs))

    def swap(value, axis, size, k):
        return lax.ppermute(value, axis, [(d, d ^ k) for d in range(size)])

    def strided(count):
        return pltpu.VMEM(((count * tiles + 1) * ROWS, TILE), jnp.float32)

    phases = [pltpu.VMEM((TILE, 4 * TILE), jnp.float32)] * STEPS + [pltpu.VMEM((TILE, 6 * TILE), jnp.bfloat16)] * STEPS
    own = pl.pallas_call(
        own_kernel,
        out_shape=[
            jax.ShapeDtypeStruct((per_dev, TERMS), jnp.bfloat16),
            jax.ShapeDtypeStruct((tiles * TERMS, 4 * TILE), jnp.bfloat16),
            jax.ShapeDtypeStruct((tiles * FEAT, TILE), jnp.bfloat16),
            jax.ShapeDtypeStruct((tiles * ROWS, 2 * TILE), jnp.float32),
            jax.ShapeDtypeStruct((ROWS, TILE), jnp.float32),
        ],
        in_specs=[vmem],
        out_specs=[vmem] * 5,
        scratch_shapes=phases + [strided(1)] * 8,
        compiler_params=params,
        cost_estimate=pl.CostEstimate(flops=tiles * 300 * TILE * TILE, bytes_accessed=2**21, transcendentals=0),
        name="own",
    )(packed)

    far = [swap(packed, "row", nrows, 2 * m) for m in range(1, halves)]
    from_row = [swap(packed, "col", ncols, k) for k in range(1, ncols)]
    joined = pl.pallas_call(
        join_kernel,
        out_shape=blocks(halves),
        in_specs=[vmem] * halves,
        out_specs=vmem,
        compiler_params=params,
        name="join",
    )(packed, *far)
    near = swap(joined, "row", nrows, 1)

    where = jnp.stack([lax.axis_index("row"), lax.axis_index("col"), pair_count[0]]).astype(jnp.int32)
    sums = pl.pallas_call(
        functools.partial(pair_kernel, nrows, ncols, tiles),
        out_shape=[blocks(1)] * ncols + [blocks(2)] * halves,
        in_specs=[smem] * 2 + [vmem] * (5 + ncols + halves),
        out_specs=[vmem] * (ncols + halves),
        scratch_shapes=[
            pltpu.VMEM((row_tiles * TILE, TERMS), jnp.bfloat16),
            pltpu.VMEM((col_tiles * TERMS, 4 * TILE), jnp.bfloat16),
            pltpu.VMEM((row_tiles * FEAT, TILE), jnp.bfloat16),
            pltpu.VMEM((col_tiles * FEAT, TILE), jnp.bfloat16),
            *[strided(ncols)] * 2,
            *[strided(nrows)] * 2,
            *[strided(ncols - 1)] * 3,
            *[strided(nrows - 1)] * 5,
            strided(ncols + nrows - 1),
            strided(ncols + nrows),
            *phases,
        ],
        compiler_params=params,
        name="pairs",
    )(where, slots, packed, *own, *from_row, *far, near)

    far_back = [swap(sums[ncols + m], "row", nrows, 2 * m) for m in range(1, halves)]
    row_back = [swap(sums[k], "col", ncols, k) for k in range(1, ncols)]
    keep, send = pl.pallas_call(
        halve_kernel,
        out_shape=[blocks(1)] * 2,
        in_specs=[vmem] * halves,
        out_specs=[vmem] * 2,
        compiler_params=params,
        name="halve",
    )(sums[ncols], *far_back)
    parts = [sums[0], keep, *row_back, swap(send, "row", nrows, 1)]
    velocity, stretching = pl.pallas_call(
        total_kernel,
        out_shape=[jax.ShapeDtypeStruct((3, per_dev), jnp.float32)] * 2,
        in_specs=[vmem] * len(parts),
        out_specs=[vmem, vmem],
        compiler_params=params,
        name="totals",
    )(*parts)
    return velocity, stretching


def solution(mesh):
    whole = ("groups", "row", "col")
    in_specs = (P(None, whole), P(None, whole), P(whole), P(whole), P(whole), P(None, whole), P(whole))
    out_specs = (P(None, whole), P(None, whole))
    return jax.shard_map(shards, mesh=mesh, in_specs=in_specs, out_specs=out_specs, check_vma=False)
```

profile of v0, /device:TPU:2, one launch (start us, length us, event | category | flops | bytes accessed | tf_op | source)
XLA Modules:
  0.0 29.3 jit_solution(8758240800120293048)
XLA Ops:
  0.6 1.5 %pack.1 = (f32[64,128]{1,0:T(8,128)S(1)}, s32[2,64]{1,0:T(2,128)S(1)}) custom-call(s32[8]{0:T(128)} %counts_hbm.1, f32[3,1024]{1,0:T(4,128)} %pos_hbm.1, f32[3,1024]{1,0:T(4,128)} %str_hbm.1, f32[1,1024]{1,0:T(1,128)} %bitcast.4, s32[1,1024]{1,0:T(1,128)} %bitcast.5, s32[2,64]{1,0:T(2,128)} %slots_hbm.1), custom_call_target="tpu_custom_call" | custom-call | tf_op jit(solution)/shard_map/pack/pallas_call | solution.py:420
  2.1 1.6 %collective-permute-start.3 = (f32[64,128]{1,0:T(8,128)S(1)}, f32[64,128]{1,0:T(8,128)S(1)}, u32[]{:S(2)}, u32[]{:S(2)}) collective-permute-start(f32[64,128]{1,0:T(8,128)S(1)} %get-tuple-element.18.block.refs_0_), channel_id=1, source_target_pairs={{0,8},{4,12},{8,0},{12,4},{1,9},{5,13},{9,1},{13,5},{2,10},{6,14},... | collective-permute-start | bytes 98312 | tf_op jit(solution)/shard_map/ppermute | solution.py:436
  3.7 3.6 %collective-permute-start.2 = (f32[64,128]{1,0:T(8,128)S(1)}, f32[64,128]{1,0:T(8,128)S(1)}, u32[]{:S(2)}, u32[]{:S(2)}) collective-permute-start(f32[64,128]{1,0:T(8,128)S(1)} %get-tuple-element.18.block.refs_0_), channel_id=1, source_target_pairs={{0,3},{1,2},{2,1},{3,0},{4,7},{5,6},{6,5},{7,4},{8,11},{9,10},{10,... | collective-permute-start | bytes 98312 | tf_op jit(solution)/shard_map/ppermute | solution.py:436
  7.3 0.0 collective-permute-start.1
  7.3 0.8 %collective-permute-start = (f32[64,128]{1,0:T(8,128)S(1)}, f32[64,128]{1,0:T(8,128)S(1)}, u32[]{:S(2)}, u32[]{:S(2)}) collective-permute-start(f32[64,128]{1,0:T(8,128)S(1)} %get-tuple-element.18.block.refs_0_), channel_id=1, source_target_pairs={{0,1},{1,0},{2,3},{3,2},{4,5},{5,4},{6,7},{7,6},{8,9},{9,8},{10,11... | collective-permute-start | bytes 98312 | tf_op jit(solution)/shard_map/ppermute | solution.py:436
  8.8 0.0 collective-permute-done.3.refs_1_.refs_9_
  8.8 0.1 collective-permute-start.4
  8.9 0.1 pad_add_fusion.where_ref
  8.9 0.9 %own.1 = (bf16[1024,64]{1,0:T(8,128)(2,1)S(1)}, bf16[512,512]{1,0:T(8,128)(2,1)S(1)}, bf16[256,128]{1,0:T(8,128)(2,1)S(1)}, f32[64,256]{1,0:T(8,128)S(1)}, f32[8,128]{1,0:T(8,128)S(1)}) custom-call(f32[64,128]{1,0:T(8,128)S(1)} %get-tuple-element.18.block.refs_0_), custom_call_target="tpu_custom_call" | custom-call | flops 39321600 | bytes 2097152 | tf_op jit(solution)/shard_map/own/pallas_call | solution.py:442
  9.9 0.0 collective-permute-done.2.refs_8_
  9.9 2.3 %collective-permute-done.1.refs_7_ = f32[64,128]{1,0:T(8,128)S(1)} collective-permute-done((f32[64,128]{1,0:T(8,128)S(1)}, f32[64,128]{1,0:T(8,128)S(1)}, u32[]{:S(2)}, u32[]{:S(2)}) %collective-permute-start.1) | collective-permute-done | bytes 32800 | tf_op jit(solution)/shard_map/ppermute | solution.py:436
  12.1 0.0 collective-permute-done.refs_6_
  12.1 0.0 collective-permute-done.4.refs_10_
  12.1 4.2 %pairs.1 = (f32[64,128]{1,0:T(8,128)S(1)}, f32[64,128]{1,0:T(8,128)S(1)}, f32[64,128]{1,0:T(8,128)S(1)}, f32[64,128]{1,0:T(8,128)S(1)}, f32[128,128]{1,0:T(8,128)S(1)}, /*index=5*/f32[128,128]{1,0:T(8,128)S(1)}) custom-call(s32[3]{0:T(128)S(1)} %pad_add_fusion.where_ref, s32[2,64]{1,0:T(2,128)S(1)} %get-tuple-element.17.slots_ref, ...), custom_call_target="tpu_custom_call" | custom-call | tf_op jit(solution)/shard_map/pairs/pallas_call | solution.py:472
  16.3 0.1 collective-permute-start.5
  16.5 3.9 %collective-permute-start.6 = (f32[64,128]{1,0:T(8,128)S(1)}, f32[64,128]{1,0:T(8,128)S(1)}, u32[]{:S(2)}, u32[]{:S(2)}) collective-permute-start(f32[64,128]{1,0:T(8,128)S(1)} %get-tuple-element.28), channel_id=1, source_target_pairs={{0,1},{1,0},{2,3},{3,2},{4,5},{5,4},{6,7},{7,6},{8,9},{9,8},{10,11... | collective-permute-start | bytes 98312 | tf_op jit(solution)/shard_map/ppermute | solution.py:436
  20.4 2.6 %collective-permute-start.7 = (f32[64,128]{1,0:T(8,128)S(1)}, f32[64,128]{1,0:T(8,128)S(1)}, u32[]{:S(2)}, u32[]{:S(2)}) collective-permute-start(f32[64,128]{1,0:T(8,128)S(1)} %get-tuple-element.29), channel_id=1, source_target_pairs={{0,2},{1,3},{2,0},{3,1},{4,6},{5,7},{6,4},{7,5},{8,10},{9,11},{10,... | collective-permute-start | bytes 98312 | tf_op jit(solution)/shard_map/ppermute | solution.py:436
  23.0 1.5 %collective-permute-start.8 = (f32[64,128]{1,0:T(8,128)S(1)}, f32[64,128]{1,0:T(8,128)S(1)}, u32[]{:S(2)}, u32[]{:S(2)}) collective-permute-start(f32[64,128]{1,0:T(8,128)S(1)} %get-tuple-element.30), channel_id=1, source_target_pairs={{0,3},{1,2},{2,1},{3,0},{4,7},{5,6},{6,5},{7,4},{8,11},{9,10},{10,... | collective-permute-start | bytes 98312 | tf_op jit(solution)/shard_map/ppermute | solution.py:436
  24.4 0.0 collective-permute-done.5.refs_1_
  24.5 0.1 collective-permute-start.9
  24.5 0.0 collective-permute-done.6.refs_2_
  24.5 0.7 %collective-permute-done.7.refs_3_ = f32[64,128]{1,0:T(8,128)S(1)} collective-permute-done((f32[64,128]{1,0:T(8,128)S(1)}, f32[64,128]{1,0:T(8,128)S(1)}, u32[]{:S(2)}, u32[]{:S(2)}) %collective-permute-start.7) | collective-permute-done | bytes 32800 | tf_op jit(solution)/shard_map/ppermute | solution.py:436
  25.2 3.5 %collective-permute-done.8.refs_4_ = f32[64,128]{1,0:T(8,128)S(1)} collective-permute-done((f32[64,128]{1,0:T(8,128)S(1)}, f32[64,128]{1,0:T(8,128)S(1)}, u32[]{:S(2)}, u32[]{:S(2)}) %collective-permute-start.8) | collective-permute-done | bytes 32800 | tf_op jit(solution)/shard_map/ppermute | solution.py:436
  28.7 0.0 collective-permute-done.9.refs_5_
  28.7 0.6 %totals.1 = (f32[3,1024]{1,0:T(4,128)}, f32[3,1024]{1,0:T(4,128)}) custom-call(f32[64,128]{1,0:T(8,128)S(1)} %get-tuple-element.24.refs_0_, f32[64,128]{1,0:T(8,128)S(1)} %get-tuple-element.27.refs_1_, f32[64,128]{1,0:T(8,128)S(1)} %collective-permute-done.6.refs_2_, f32[64,128]{1,0:T(8,128)S(1)} %collective-permute-done.7.refs_3_, ...), custom_call_target="tpu_custom_call" | custom-call | tf_op jit(solution)/shard_map/totals/pallas_call | solution.py:505
  (2 shorter events, 0.0 us)
Async XLA Ops:
  2.1 6.6 %collective-permute-start.3 = (f32[64,128]{1,0:T(8,128)S(1)}, f32[64,128]{1,0:T(8,128)S(1)}, u32[]{:S(2)}, u32[]{:S(2)}) collective-permute-start(f32[64,128]{1,0:T(8,128)S(1)} %get-tuple-element.18.block.refs_0_), channel_id=1, source_target_pairs={{0,8},{4,12},{8,0},{12,4},{1,9},{5,13},{9,1},{13,5},{2,10},{6,14},... | collective-permute-start | bytes 98312 | tf_op jit(solution)/shard_map/ppermute | solution.py:436
  3.7 6.1 %collective-permute-start.2 = (f32[64,128]{1,0:T(8,128)S(1)}, f32[64,128]{1,0:T(8,128)S(1)}, u32[]{:S(2)}, u32[]{:S(2)}) collective-permute-start(f32[64,128]{1,0:T(8,128)S(1)} %get-tuple-element.18.block.refs_0_), channel_id=1, source_target_pairs={{0,3},{1,2},{2,1},{3,0},{4,7},{5,6},{6,5},{7,4},{8,11},{9,10},{10,... | collective-permute-start | bytes 98312 | tf_op jit(solution)/shard_map/ppermute | solution.py:436
  7.3 4.8 %collective-permute-start.1 = (f32[64,128]{1,0:T(8,128)S(1)}, f32[64,128]{1,0:T(8,128)S(1)}, u32[]{:S(2)}, u32[]{:S(2)}) collective-permute-start(f32[64,128]{1,0:T(8,128)S(1)} %get-tuple-element.18.block.refs_0_), channel_id=1, source_target_pairs={{0,2},{1,3},{2,0},{3,1},{4,6},{5,7},{6,4},{7,5},{8,10},{9,11},{10,... | collective-permute-start | bytes 98312 | tf_op jit(solution)/shard_map/ppermute | solution.py:436
  7.3 4.8 %collective-permute-start = (f32[64,128]{1,0:T(8,128)S(1)}, f32[64,128]{1,0:T(8,128)S(1)}, u32[]{:S(2)}, u32[]{:S(2)}) collective-permute-start(f32[64,128]{1,0:T(8,128)S(1)} %get-tuple-element.18.block.refs_0_), channel_id=1, source_target_pairs={{0,1},{1,0},{2,3},{3,2},{4,5},{5,4},{6,7},{7,6},{8,9},{9,8},{10,11... | collective-permute-start | bytes 98312 | tf_op jit(solution)/shard_map/ppermute | solution.py:436
  8.8 3.4 %collective-permute-start.4 = (f32[128,128]{1,0:T(8,128)S(1)}, f32[128,128]{1,0:T(8,128)S(1)}, u32[]{:S(2)}, u32[]{:S(2)}) collective-permute-start(f32[128,128]{1,0:T(8,128)S(1)} %join.1), channel_id=1, source_target_pairs={{0,4},{4,0},{8,12},{12,8},{1,5},{5,1},{9,13},{13,9},{2,6},{6,2},{1... | collective-permute-start | bytes 196616 | tf_op jit(solution)/shard_map/ppermute | solution.py:436
  16.3 8.1 %collective-permute-start.5 = (f32[128,128]{1,0:T(8,128)S(1)}, f32[128,128]{1,0:T(8,128)S(1)}, u32[]{:S(2)}, u32[]{:S(2)}) collective-permute-start(f32[128,128]{1,0:T(8,128)S(1)} %get-tuple-element.26), channel_id=1, source_target_pairs={{0,8},{4,12},{8,0},{12,4},{1,9},{5,13},{9,1},{13,5},{2,10},{6,14},... | collective-permute-start | bytes 196616 | tf_op jit(solution)/shard_map/ppermute | solution.py:436
  16.5 8.1 %collective-permute-start.6 = (f32[64,128]{1,0:T(8,128)S(1)}, f32[64,128]{1,0:T(8,128)S(1)}, u32[]{:S(2)}, u32[]{:S(2)}) collective-permute-start(f32[64,128]{1,0:T(8,128)S(1)} %get-tuple-element.28), channel_id=1, source_target_pairs={{0,1},{1,0},{2,3},{3,2},{4,5},{5,4},{6,7},{7,6},{8,9},{9,8},{10,11... | collective-permute-start | bytes 98312 | tf_op jit(solution)/shard_map/ppermute | solution.py:436
  20.4 4.8 %collective-permute-start.7 = (f32[64,128]{1,0:T(8,128)S(1)}, f32[64,128]{1,0:T(8,128)S(1)}, u32[]{:S(2)}, u32[]{:S(2)}) collective-permute-start(f32[64,128]{1,0:T(8,128)S(1)} %get-tuple-element.29), channel_id=1, source_target_pairs={{0,2},{1,3},{2,0},{3,1},{4,6},{5,7},{6,4},{7,5},{8,10},{9,11},{10,... | collective-permute-start | bytes 98312 | tf_op jit(solution)/shard_map/ppermute | solution.py:436
  23.0 5.7 %collective-permute-start.8 = (f32[64,128]{1,0:T(8,128)S(1)}, f32[64,128]{1,0:T(8,128)S(1)}, u32[]{:S(2)}, u32[]{:S(2)}) collective-permute-start(f32[64,128]{1,0:T(8,128)S(1)} %get-tuple-element.30), channel_id=1, source_target_pairs={{0,3},{1,2},{2,1},{3,0},{4,7},{5,6},{6,5},{7,4},{8,11},{9,10},{10,... | collective-permute-start | bytes 98312 | tf_op jit(solution)/shard_map/ppermute | solution.py:436
  24.5 4.2 %collective-permute-start.9 = (f32[64,128]{1,0:T(8,128)S(1)}, f32[64,128]{1,0:T(8,128)S(1)}, u32[]{:S(2)}, u32[]{:S(2)}) collective-permute-start(f32[64,128]{1,0:T(8,128)S(1)} %get-tuple-element.31), channel_id=1, source_target_pairs={{0,4},{4,0},{8,12},{12,8},{1,5},{5,1},{9,13},{13,9},{2,6},{6,2},{1... | collective-permute-start | bytes 98312 | tf_op jit(solution)/shard_map/ppermute | solution.py:436
where the time goes:
time: 29.6 us; the launch traced here: 29.3 us
  starting transfers between devices  14.2 us (48%)
  Pallas kernels  7.26 us (25%)
  waiting for transfers between devices  6.45 us (22%)
  between operations  1.35 us (5%)
    ppermute x10, starting transfers between devices, swap(): return lax.ppermute(value, axis, [(d, d ^ k) for d in range(size)])  14.2 us
    ppermute x10, waiting for transfers between devices, swap(): return lax.ppermute(value, axis, [(d, d ^ k) for d in range(size)])  6.45 us
    pallas_call x1, Pallas kernels, shards(): pl.pallas_call(functools.partial(pair_kernel, nrows, ncols, tiles), out_s...  4.19 us
    pallas_call x1, Pallas kernels, shards(): pl.pallas_call(pack_kernel, out_shape=[blocks(1), jax.ShapeDtypeStruct(pa...  1.5 us
    pallas_call x1, Pallas kernels, shards(): pl.pallas_call(own_kernel, out_shape=[jax.ShapeDtypeStruct((per_dev, TERM...  0.92 us
    pallas_call x1, Pallas kernels, shards(): pl.pallas_call(total_kernel, out_shape=[jax.ShapeDtypeStruct((3, per_dev)...  0.63 us
  transfers between devices with their start and end apart: 10, of which 3 were waited for; matrix products, arithmetic and copies ran while one was open for 0% of the time, Pallas kernels for 3%

commit v1 on v0

--- a/solution.py
+++ b/solution.py
@@ -322,7 +322,7 @@
             right[term_at(tile), :] = source_side(*staged[1:], rows)
         return carry
 
-    lax.fori_loop(0, tiles, prepare, 0, unroll=2)
+    lax.fori_loop(0, tiles, prepare, 0, unroll=4)
 
     last = slots_ref.shape[1] - 1
 
@@ -492,7 +492,7 @@
     )(where, slots, packed, *own, *from_row, *far, near)
 
     far_back = [swap(sums[ncols + m], "row", nrows, 2 * m) for m in range(1, halves)]
-    row_back = [swap(sums[k], "col", ncols, k) for k in range(1, ncols)]
+    row_back = [swap(sums[k], "col", ncols, k) for k in reversed(range(1, ncols))]
     keep, send = pl.pallas_call(
         halve_kernel,
         out_shape=[blocks(1)] * 2,

time: 29.6 us -> 28.8 us (0.973)
  the two profiles are of different devices: /device:TPU:2 before, /device:TPU:0 now
where the time goes in v1:
time: 28.8 us; the launch traced here: 28.4 us
  starting transfers between devices  13.3 us (46%)
  Pallas kernels  7.59 us (26%)
  waiting for transfers between devices  6.11 us (21%)
  between operations  1.33 us (5%)
    ppermute x10, starting transfers between devices, swap(): return lax.ppermute(value, axis, [(d, d ^ k) for d in range(size)])  13.3 us
    ppermute x10, waiting for transfers between devices, swap(): return lax.ppermute(value, axis, [(d, d ^ k) for d in range(size)])  6.11 us
    pallas_call x1, Pallas kernels, shards(): pl.pallas_call(functools.partial(pair_kernel, nrows, ncols, tiles), out_s...  4.53 us
    pallas_call x1, Pallas kernels, shards(): pl.pallas_call(pack_kernel, out_shape=[blocks(1), jax.ShapeDtypeStruct(pa...  1.5 us
    pallas_call x1, Pallas kernels, shards(): pl.pallas_call(own_kernel, out_shape=[jax.ShapeDtypeStruct((per_dev, TERM...  0.92 us
    pallas_call x1, Pallas kernels, shards(): pl.pallas_call(total_kernel, out_shape=[jax.ShapeDtypeStruct((3, per_dev)...  0.63 us
  transfers between devices with their start and end apart: 10, of which 4 were waited for; matrix products, arithmetic and copies ran while one was open for 0% of the time, Pallas kernels for 3%

profile of v1, /device:TPU:0, one launch (start us, length us, event | category | flops | bytes accessed | tf_op | source)
XLA Modules:
  0.0 28.4 jit_solution(16272026613730667657)
XLA Ops:
  0.6 1.5 %pack.1 = (f32[64,128]{1,0:T(8,128)S(1)}, s32[2,64]{1,0:T(2,128)S(1)}) custom-call(s32[8]{0:T(128)} %counts_hbm.1, f32[3,1024]{1,0:T(4,128)} %pos_hbm.1, f32[3,1024]{1,0:T(4,128)} %str_hbm.1, f32[1,1024]{1,0:T(1,128)} %bitcast.4, s32[1,1024]{1,0:T(1,128)} %bitcast.5, s32[2,64]{1,0:T(2,128)} %slots_hbm.1), custom_call_target="tpu_custom_call" | custom-call | tf_op jit(solution)/shard_map/pack/pallas_call | solution.py:420
  2.1 3.0 %collective-permute-start.3 = (f32[64,128]{1,0:T(8,128)S(1)}, f32[64,128]{1,0:T(8,128)S(1)}, u32[]{:S(2)}, u32[]{:S(2)}) collective-permute-start(f32[64,128]{1,0:T(8,128)S(1)} %get-tuple-element.18.block.refs_0_), channel_id=1, source_target_pairs={{0,8},{4,12},{8,0},{12,4},{1,9},{5,13},{9,1},{13,5},{2,10},{6,14},... | collective-permute-start | bytes 98312 | tf_op jit(solution)/shard_map/ppermute | solution.py:436
  5.2 3.6 %collective-permute-start.2 = (f32[64,128]{1,0:T(8,128)S(1)}, f32[64,128]{1,0:T(8,128)S(1)}, u32[]{:S(2)}, u32[]{:S(2)}) collective-permute-start(f32[64,128]{1,0:T(8,128)S(1)} %get-tuple-element.18.block.refs_0_), channel_id=1, source_target_pairs={{0,3},{1,2},{2,1},{3,0},{4,7},{5,6},{6,5},{7,4},{8,11},{9,10},{10,... | collective-permute-start | bytes 98312 | tf_op jit(solution)/shard_map/ppermute | solution.py:436
  8.8 0.0 collective-permute-start.1
  8.8 0.8 %collective-permute-start = (f32[64,128]{1,0:T(8,128)S(1)}, f32[64,128]{1,0:T(8,128)S(1)}, u32[]{:S(2)}, u32[]{:S(2)}) collective-permute-start(f32[64,128]{1,0:T(8,128)S(1)} %get-tuple-element.18.block.refs_0_), channel_id=1, source_target_pairs={{0,1},{1,0},{2,3},{3,2},{4,5},{5,4},{6,7},{7,6},{8,9},{9,8},{10,11... | collective-permute-start | bytes 98312 | tf_op jit(solution)/shard_map/ppermute | solution.py:436
  10.2 0.0 collective-permute-done.3.refs_1_.refs_9_
  10.2 0.1 collective-permute-start.4
  10.3 0.1 pad_add_fusion.where_ref
  10.4 0.9 %own.1 = (bf16[1024,64]{1,0:T(8,128)(2,1)S(1)}, bf16[512,512]{1,0:T(8,128)(2,1)S(1)}, bf16[256,128]{1,0:T(8,128)(2,1)S(1)}, f32[64,256]{1,0:T(8,128)S(1)}, f32[8,128]{1,0:T(8,128)S(1)}) custom-call(f32[64,128]{1,0:T(8,128)S(1)} %get-tuple-element.18.block.refs_0_), custom_call_target="tpu_custom_call" | custom-call | flops 39321600 | bytes 2097152 | tf_op jit(solution)/shard_map/own/pallas_call | solution.py:442
  11.3 0.0 collective-permute-done.2.refs_8_
  11.3 2.3 %collective-permute-done.1.refs_7_ = f32[64,128]{1,0:T(8,128)S(1)} collective-permute-done((f32[64,128]{1,0:T(8,128)S(1)}, f32[64,128]{1,0:T(8,128)S(1)}, u32[]{:S(2)}, u32[]{:S(2)}) %collective-permute-start.1) | collective-permute-done | bytes 32800 | tf_op jit(solution)/shard_map/ppermute | solution.py:436
  13.6 0.0 collective-permute-done.refs_6_
  13.6 0.0 collective-permute-done.4.refs_10_
  13.6 4.5 %pairs.1 = (f32[64,128]{1,0:T(8,128)S(1)}, f32[64,128]{1,0:T(8,128)S(1)}, f32[64,128]{1,0:T(8,128)S(1)}, f32[64,128]{1,0:T(8,128)S(1)}, f32[128,128]{1,0:T(8,128)S(1)}, /*index=5*/f32[128,128]{1,0:T(8,128)S(1)}) custom-call(s32[3]{0:T(128)S(1)} %pad_add_fusion.where_ref, s32[2,64]{1,0:T(2,128)S(1)} %get-tuple-element.17.slots_ref, ...), custom_call_target="tpu_custom_call" | custom-call | tf_op jit(solution)/shard_map/pairs/pallas_call | solution.py:472
  18.1 0.6 %collective-permute-start.5 = (f32[128,128]{1,0:T(8,128)S(1)}, f32[128,128]{1,0:T(8,128)S(1)}, u32[]{:S(2)}, u32[]{:S(2)}) collective-permute-start(f32[128,128]{1,0:T(8,128)S(1)} %get-tuple-element.26), channel_id=1, source_target_pairs={{0,8},{4,12},{8,0},{12,4},{1,9},{5,13},{9,1},{13,5},{2,10},{6,14},... | collective-permute-start | bytes 196616 | tf_op jit(solution)/shard_map/ppermute | solution.py:436
  18.7 0.2 collective-permute-start.6
  18.9 4.6 %collective-permute-start.7 = (f32[64,128]{1,0:T(8,128)S(1)}, f32[64,128]{1,0:T(8,128)S(1)}, u32[]{:S(2)}, u32[]{:S(2)}) collective-permute-start(f32[64,128]{1,0:T(8,128)S(1)} %get-tuple-element.29), channel_id=1, source_target_pairs={{0,2},{1,3},{2,0},{3,1},{4,6},{5,7},{6,4},{7,5},{8,10},{9,11},{10,... | collective-permute-start | bytes 98312 | tf_op jit(solution)/shard_map/ppermute | solution.py:436
  23.5 0.0 collective-permute-start.8
  23.5 0.0 collective-permute-done.5.refs_1_
  23.6 0.4 %collective-permute-start.9 = (f32[64,128]{1,0:T(8,128)S(1)}, f32[64,128]{1,0:T(8,128)S(1)}, u32[]{:S(2)}, u32[]{:S(2)}) collective-permute-start(f32[64,128]{1,0:T(8,128)S(1)} %get-tuple-element.31), channel_id=1, source_target_pairs={{0,4},{4,0},{8,12},{12,8},{1,5},{5,1},{9,13},{13,9},{2,6},{6,2},{1... | collective-permute-start | bytes 98312 | tf_op jit(solution)/shard_map/ppermute | solution.py:436
  24.0 0.4 %collective-permute-done.6.refs_2_ = f32[64,128]{1,0:T(8,128)S(1)} collective-permute-done((f32[64,128]{1,0:T(8,128)S(1)}, f32[64,128]{1,0:T(8,128)S(1)}, u32[]{:S(2)}, u32[]{:S(2)}) %collective-permute-start.6) | collective-permute-done | bytes 32800 | tf_op jit(solution)/shard_map/ppermute | solution.py:436
  24.4 2.2 %collective-permute-done.7.refs_3_ = f32[64,128]{1,0:T(8,128)S(1)} collective-permute-done((f32[64,128]{1,0:T(8,128)S(1)}, f32[64,128]{1,0:T(8,128)S(1)}, u32[]{:S(2)}, u32[]{:S(2)}) %collective-permute-start.7) | collective-permute-done | bytes 32800 | tf_op jit(solution)/shard_map/ppermute | solution.py:436
  26.6 1.2 %collective-permute-done.8.refs_4_ = f32[64,128]{1,0:T(8,128)S(1)} collective-permute-done((f32[64,128]{1,0:T(8,128)S(1)}, f32[64,128]{1,0:T(8,128)S(1)}, u32[]{:S(2)}, u32[]{:S(2)}) %collective-permute-start.8) | collective-permute-done | bytes 32800 | tf_op jit(solution)/shard_map/ppermute | solution.py:436
  27.8 0.0 collective-permute-done.9.refs_5_
  27.8 0.6 %totals.1 = (f32[3,1024]{1,0:T(4,128)}, f32[3,1024]{1,0:T(4,128)}) custom-call(f32[64,128]{1,0:T(8,128)S(1)} %get-tuple-element.24.refs_0_, f32[64,128]{1,0:T(8,128)S(1)} %get-tuple-element.27.refs_1_, f32[64,128]{1,0:T(8,128)S(1)} %collective-permute-done.6.refs_2_, f32[64,128]{1,0:T(8,128)S(1)} %collective-permute-done.7.refs_3_, ...), custom_call_target="tpu_custom_call" | custom-call | tf_op jit(solution)/shard_map/totals/pallas_call | solution.py:505
  (2 shorter events, 0.0 us)
Async XLA Ops:
  2.1 8.1 %collective-permute-start.3 = (f32[64,128]{1,0:T(8,128)S(1)}, f32[64,128]{1,0:T(8,128)S(1)}, u32[]{:S(2)}, u32[]{:S(2)}) collective-permute-start(f32[64,128]{1,0:T(8,128)S(1)} %get-tuple-element.18.block.refs_0_), channel_id=1, source_target_pairs={{0,8},{4,12},{8,0},{12,4},{1,9},{5,13},{9,1},{13,5},{2,10},{6,14},... | collective-permute-start | bytes 98312 | tf_op jit(solution)/shard_map/ppermute | solution.py:436
  5.2 6.1 %collective-permute-start.2 = (f32[64,128]{1,0:T(8,128)S(1)}, f32[64,128]{1,0:T(8,128)S(1)}, u32[]{:S(2)}, u32[]{:S(2)}) collective-permute-start(f32[64,128]{1,0:T(8,128)S(1)} %get-tuple-element.18.block.refs_0_), channel_id=1, source_target_pairs={{0,3},{1,2},{2,1},{3,0},{4,7},{5,6},{6,5},{7,4},{8,11},{9,10},{10,... | collective-permute-start | bytes 98312 | tf_op jit(solution)/shard_map/ppermute | solution.py:436
  8.8 4.8 %collective-permute-start.1 = (f32[64,128]{1,0:T(8,128)S(1)}, f32[64,128]{1,0:T(8,128)S(1)}, u32[]{:S(2)}, u32[]{:S(2)}) collective-permute-start(f32[64,128]{1,0:T(8,128)S(1)} %get-tuple-element.18.block.refs_0_), channel_id=1, source_target_pairs={{0,2},{1,3},{2,0},{3,1},{4,6},{5,7},{6,4},{7,5},{8,10},{9,11},{10,... | collective-permute-start | bytes 98312 | tf_op jit(solution)/shard_map/ppermute | solution.py:436
  8.8 4.8 %collective-permute-start = (f32[64,128]{1,0:T(8,128)S(1)}, f32[64,128]{1,0:T(8,128)S(1)}, u32[]{:S(2)}, u32[]{:S(2)}) collective-permute-start(f32[64,128]{1,0:T(8,128)S(1)} %get-tuple-element.18.block.refs_0_), channel_id=1, source_target_pairs={{0,1},{1,0},{2,3},{3,2},{4,5},{5,4},{6,7},{7,6},{8,9},{9,8},{10,11... | collective-permute-start | bytes 98312 | tf_op jit(solution)/shard_map/ppermute | solution.py:436
  10.2 3.4 %collective-permute-start.4 = (f32[128,128]{1,0:T(8,128)S(1)}, f32[128,128]{1,0:T(8,128)S(1)}, u32[]{:S(2)}, u32[]{:S(2)}) collective-permute-start(f32[128,128]{1,0:T(8,128)S(1)} %join.1), channel_id=1, source_target_pairs={{0,4},{4,0},{8,12},{12,8},{1,5},{5,1},{9,13},{13,9},{2,6},{6,2},{1... | collective-permute-start | bytes 196616 | tf_op jit(solution)/shard_map/ppermute | solution.py:436
  18.1 5.4 %collective-permute-start.5 = (f32[128,128]{1,0:T(8,128)S(1)}, f32[128,128]{1,0:T(8,128)S(1)}, u32[]{:S(2)}, u32[]{:S(2)}) collective-permute-start(f32[128,128]{1,0:T(8,128)S(1)} %get-tuple-element.26), channel_id=1, source_target_pairs={{0,8},{4,12},{8,0},{12,4},{1,9},{5,13},{9,1},{13,5},{2,10},{6,14},... | collective-permute-start | bytes 196616 | tf_op jit(solution)/shard_map/ppermute | solution.py:436
  18.7 5.7 %collective-permute-start.6 = (f32[64,128]{1,0:T(8,128)S(1)}, f32[64,128]{1,0:T(8,128)S(1)}, u32[]{:S(2)}, u32[]{:S(2)}) collective-permute-start(f32[64,128]{1,0:T(8,128)S(1)} %get-tuple-element.28), channel_id=1, source_target_pairs={{0,3},{1,2},{2,1},{3,0},{4,7},{5,6},{6,5},{7,4},{8,11},{9,10},{10,... | collective-permute-start | bytes 98312 | tf_op jit(solution)/shard_map/ppermute | solution.py:436
  18.9 7.7 %collective-permute-start.7 = (f32[64,128]{1,0:T(8,128)S(1)}, f32[64,128]{1,0:T(8,128)S(1)}, u32[]{:S(2)}, u32[]{:S(2)}) collective-permute-start(f32[64,128]{1,0:T(8,128)S(1)} %get-tuple-element.29), channel_id=1, source_target_pairs={{0,2},{1,3},{2,0},{3,1},{4,6},{5,7},{6,4},{7,5},{8,10},{9,11},{10,... | collective-permute-start | bytes 98312 | tf_op jit(solution)/shard_map/ppermute | solution.py:436
  23.5 4.2 %collective-permute-start.8 = (f32[64,128]{1,0:T(8,128)S(1)}, f32[64,128]{1,0:T(8,128)S(1)}, u32[]{:S(2)}, u32[]{:S(2)}) collective-permute-start(f32[64,128]{1,0:T(8,128)S(1)} %get-tuple-element.30), channel_id=1, source_target_pairs={{0,1},{1,0},{2,3},{3,2},{4,5},{5,4},{6,7},{7,6},{8,9},{9,8},{10,11... | collective-permute-start | bytes 98312 | tf_op jit(solution)/shard_map/ppermute | solution.py:436
  23.6 4.2 %collective-permute-start.9 = (f32[64,128]{1,0:T(8,128)S(1)}, f32[64,128]{1,0:T(8,128)S(1)}, u32[]{:S(2)}, u32[]{:S(2)}) collective-permute-start(f32[64,128]{1,0:T(8,128)S(1)} %get-tuple-element.31), channel_id=1, source_target_pairs={{0,4},{4,0},{8,12},{12,8},{1,5},{5,1},{9,13},{13,9},{2,6},{6,2},{1... | collective-permute-start | bytes 98312 | tf_op jit(solution)/shard_map/ppermute | solution.py:436

commit v2 on v1

--- a/solution.py
+++ b/solution.py
@@ -10,7 +10,7 @@
 
 TILE = 128
 ROWS = 8
-STEPS = 4
+STEPS = 8
 LEAD = 2
 FEAT = 32
 TERMS = 64
@@ -322,7 +322,7 @@
             right[term_at(tile), :] = source_side(*staged[1:], rows)
         return carry
 
-    lax.fori_loop(0, tiles, prepare, 0, unroll=4)
+    lax.fori_loop(0, tiles, prepare, 0, unroll=8)
 
     last = slots_ref.shape[1] - 1
 

time: 28.8 us -> 27.1 us (0.941); the launches traced: 28.4 us -> 27.2 us
  Pallas kernels: 7.59 us -> 7 us
  waiting for transfers between devices: 6.11 us -> 5.62 us
    pallas_call x1, Pallas kernels: 4.53 us -> 3.93 us  [shards(): pl.pallas_call(functools.partial(pair_kernel, nrows, ncols, tiles), out_s...]
    ppermute x10, waiting for transfers between devices: 6.11 us -> 5.62 us  [swap(): return lax.ppermute(value, axis, [(d, d ^ k) for d in range(size)])]
where the time goes in v2:
time: 27.1 us; the launch traced here: 27.2 us
  starting transfers between devices  13.2 us (49%)
  Pallas kernels  7 us (26%)
  waiting for transfers between devices  5.62 us (21%)
  between operations  1.35 us (5%)
    ppermute x10, starting transfers between devices, swap(): return lax.ppermute(value, axis, [(d, d ^ k) for d in range(size)])  13.2 us
    ppermute x10, waiting for transfers between devices, swap(): return lax.ppermute(value, axis, [(d, d ^ k) for d in range(size)])  5.62 us
    pallas_call x1, Pallas kernels, shards(): pl.pallas_call(functools.partial(pair_kernel, nrows, ncols, tiles), out_s...  3.93 us
    pallas_call x1, Pallas kernels, shards(): pl.pallas_call(pack_kernel, out_shape=[blocks(1), jax.ShapeDtypeStruct(pa...  1.5 us
    pallas_call x1, Pallas kernels, shards(): pl.pallas_call(own_kernel, out_shape=[jax.ShapeDtypeStruct((per_dev, TERM...  0.92 us
    pallas_call x1, Pallas kernels, shards(): pl.pallas_call(total_kernel, out_shape=[jax.ShapeDtypeStruct((3, per_dev)...  0.63 us
  transfers between devices with their start and end apart: 10, of which 4 were waited for; matrix products, arithmetic and copies ran while one was open for 0% of the time, Pallas kernels for 3%

profile of v2, /device:TPU:0, one launch (start us, length us, event | category | flops | bytes accessed | tf_op | source)
XLA Modules:
  0.0 27.2 jit_solution(12817389238021794318)
XLA Ops:
  0.6 1.5 %pack.1 = (f32[64,128]{1,0:T(8,128)S(1)}, s32[2,64]{1,0:T(2,128)S(1)}) custom-call(s32[8]{0:T(128)} %counts_hbm.1, f32[3,1024]{1,0:T(4,128)} %pos_hbm.1, f32[3,1024]{1,0:T(4,128)} %str_hbm.1, f32[1,1024]{1,0:T(1,128)} %bitcast.4, s32[1,1024]{1,0:T(1,128)} %bitcast.5, s32[2,64]{1,0:T(2,128)} %slots_hbm.1), custom_call_target="tpu_custom_call" | custom-call | tf_op jit(solution)/shard_map/pack/pallas_call | solution.py:420
  2.1 3.0 %collective-permute-start.3 = (f32[64,128]{1,0:T(8,128)S(1)}, f32[64,128]{1,0:T(8,128)S(1)}, u32[]{:S(2)}, u32[]{:S(2)}) collective-permute-start(f32[64,128]{1,0:T(8,128)S(1)} %get-tuple-element.18.block.refs_0_), channel_id=1, source_target_pairs={{0,8},{4,12},{8,0},{12,4},{1,9},{5,13},{9,1},{13,5},{2,10},{6,14},... | collective-permute-start | bytes 98312 | tf_op jit(solution)/shard_map/ppermute | solution.py:436
  5.2 3.6 %collective-permute-start.2 = (f32[64,128]{1,0:T(8,128)S(1)}, f32[64,128]{1,0:T(8,128)S(1)}, u32[]{:S(2)}, u32[]{:S(2)}) collective-permute-start(f32[64,128]{1,0:T(8,128)S(1)} %get-tuple-element.18.block.refs_0_), channel_id=1, source_target_pairs={{0,3},{1,2},{2,1},{3,0},{4,7},{5,6},{6,5},{7,4},{8,11},{9,10},{10,... | collective-permute-start | bytes 98312 | tf_op jit(solution)/shard_map/ppermute | solution.py:436
  8.8 0.0 collective-permute-start.1
  8.8 0.8 %collective-permute-start = (f32[64,128]{1,0:T(8,128)S(1)}, f32[64,128]{1,0:T(8,128)S(1)}, u32[]{:S(2)}, u32[]{:S(2)}) collective-permute-start(f32[64,128]{1,0:T(8,128)S(1)} %get-tuple-element.18.block.refs_0_), channel_id=1, source_target_pairs={{0,1},{1,0},{2,3},{3,2},{4,5},{5,4},{6,7},{7,6},{8,9},{9,8},{10,11... | collective-permute-start | bytes 98312 | tf_op jit(solution)/shard_map/ppermute | solution.py:436
  10.2 0.0 collective-permute-done.3.refs_1_.refs_9_
  10.2 0.1 collective-permute-start.4
  10.3 0.1 pad_add_fusion.where_ref
  10.4 0.9 %own.1 = (bf16[1024,64]{1,0:T(8,128)(2,1)S(1)}, bf16[512,512]{1,0:T(8,128)(2,1)S(1)}, bf16[256,128]{1,0:T(8,128)(2,1)S(1)}, f32[64,256]{1,0:T(8,128)S(1)}, f32[8,128]{1,0:T(8,128)S(1)}) custom-call(f32[64,128]{1,0:T(8,128)S(1)} %get-tuple-element.18.block.refs_0_), custom_call_target="tpu_custom_call" | custom-call | flops 39321600 | bytes 2097152 | tf_op jit(solution)/shard_map/own/pallas_call | solution.py:442
  11.3 0.0 collective-permute-done.2.refs_8_
  11.3 2.3 %collective-permute-done.1.refs_7_ = f32[64,128]{1,0:T(8,128)S(1)} collective-permute-done((f32[64,128]{1,0:T(8,128)S(1)}, f32[64,128]{1,0:T(8,128)S(1)}, u32[]{:S(2)}, u32[]{:S(2)}) %collective-permute-start.1) | collective-permute-done | bytes 32800 | tf_op jit(solution)/shard_map/ppermute | solution.py:436
  13.6 0.0 collective-permute-done.refs_6_
  13.6 0.0 collective-permute-done.4.refs_10_
  13.6 3.9 %pairs.1 = (f32[64,128]{1,0:T(8,128)S(1)}, f32[64,128]{1,0:T(8,128)S(1)}, f32[64,128]{1,0:T(8,128)S(1)}, f32[64,128]{1,0:T(8,128)S(1)}, f32[128,128]{1,0:T(8,128)S(1)}, /*index=5*/f32[128,128]{1,0:T(8,128)S(1)}) custom-call(s32[3]{0:T(128)S(1)} %pad_add_fusion.where_ref, s32[2,64]{1,0:T(2,128)S(1)} %get-tuple-element.17.slots_ref, ...), custom_call_target="tpu_custom_call" | custom-call | tf_op jit(solution)/shard_map/pairs/pallas_call | solution.py:472
  17.5 0.1 collective-permute-start.5
  17.6 1.6 %collective-permute-start.6 = (f32[64,128]{1,0:T(8,128)S(1)}, f32[64,128]{1,0:T(8,128)S(1)}, u32[]{:S(2)}, u32[]{:S(2)}) collective-permute-start(f32[64,128]{1,0:T(8,128)S(1)} %get-tuple-element.28), channel_id=1, source_target_pairs={{0,3},{1,2},{2,1},{3,0},{4,7},{5,6},{6,5},{7,4},{8,11},{9,10},{10,... | collective-permute-start | bytes 98312 | tf_op jit(solution)/shard_map/ppermute | solution.py:436
  19.2 3.4 %collective-permute-start.7 = (f32[64,128]{1,0:T(8,128)S(1)}, f32[64,128]{1,0:T(8,128)S(1)}, u32[]{:S(2)}, u32[]{:S(2)}) collective-permute-start(f32[64,128]{1,0:T(8,128)S(1)} %get-tuple-element.29), channel_id=1, source_target_pairs={{0,2},{1,3},{2,0},{3,1},{4,6},{5,7},{6,4},{7,5},{8,10},{9,11},{10,... | collective-permute-start | bytes 98312 | tf_op jit(solution)/shard_map/ppermute | solution.py:436
  22.7 0.5 %collective-permute-start.8 = (f32[64,128]{1,0:T(8,128)S(1)}, f32[64,128]{1,0:T(8,128)S(1)}, u32[]{:S(2)}, u32[]{:S(2)}) collective-permute-start(f32[64,128]{1,0:T(8,128)S(1)} %get-tuple-element.30), channel_id=1, source_target_pairs={{0,1},{1,0},{2,3},{3,2},{4,5},{5,4},{6,7},{7,6},{8,9},{9,8},{10,11... | collective-permute-start | bytes 98312 | tf_op jit(solution)/shard_map/ppermute | solution.py:436
  23.2 0.0 collective-permute-done.5.refs_1_
  23.2 0.1 collective-permute-start.9
  23.3 0.4 %collective-permute-done.6.refs_2_ = f32[64,128]{1,0:T(8,128)S(1)} collective-permute-done((f32[64,128]{1,0:T(8,128)S(1)}, f32[64,128]{1,0:T(8,128)S(1)}, u32[]{:S(2)}, u32[]{:S(2)}) %collective-permute-start.6) | collective-permute-done | bytes 32800 | tf_op jit(solution)/shard_map/ppermute | solution.py:436
  23.6 1.4 %collective-permute-done.7.refs_3_ = f32[64,128]{1,0:T(8,128)S(1)} collective-permute-done((f32[64,128]{1,0:T(8,128)S(1)}, f32[64,128]{1,0:T(8,128)S(1)}, u32[]{:S(2)}, u32[]{:S(2)}) %collective-permute-start.7) | collective-permute-done | bytes 32800 | tf_op jit(solution)/shard_map/ppermute | solution.py:436
  25.0 1.6 %collective-permute-done.8.refs_4_ = f32[64,128]{1,0:T(8,128)S(1)} collective-permute-done((f32[64,128]{1,0:T(8,128)S(1)}, f32[64,128]{1,0:T(8,128)S(1)}, u32[]{:S(2)}, u32[]{:S(2)}) %collective-permute-start.8) | collective-permute-done | bytes 32800 | tf_op jit(solution)/shard_map/ppermute | solution.py:436
  26.6 0.0 collective-permute-done.9.refs_5_
  26.6 0.6 %totals.1 = (f32[3,1024]{1,0:T(4,128)}, f32[3,1024]{1,0:T(4,128)}) custom-call(f32[64,128]{1,0:T(8,128)S(1)} %get-tuple-element.24.refs_0_, f32[64,128]{1,0:T(8,128)S(1)} %get-tuple-element.27.refs_1_, f32[64,128]{1,0:T(8,128)S(1)} %collective-permute-done.6.refs_2_, f32[64,128]{1,0:T(8,128)S(1)} %collective-permute-done.7.refs_3_, ...), custom_call_target="tpu_custom_call" | custom-call | tf_op jit(solution)/shard_map/totals/pallas_call | solution.py:505
  (2 shorter events, 0.0 us)
Async XLA Ops:
  2.1 8.1 %collective-permute-start.3 = (f32[64,128]{1,0:T(8,128)S(1)}, f32[64,128]{1,0:T(8,128)S(1)}, u32[]{:S(2)}, u32[]{:S(2)}) collective-permute-start(f32[64,128]{1,0:T(8,128)S(1)} %get-tuple-element.18.block.refs_0_), channel_id=1, source_target_pairs={{0,8},{4,12},{8,0},{12,4},{1,9},{5,13},{9,1},{13,5},{2,10},{6,14},... | collective-permute-start | bytes 98312 | tf_op jit(solution)/shard_map/ppermute | solution.py:436
  5.2 6.1 %collective-permute-start.2 = (f32[64,128]{1,0:T(8,128)S(1)}, f32[64,128]{1,0:T(8,128)S(1)}, u32[]{:S(2)}, u32[]{:S(2)}) collective-permute-start(f32[64,128]{1,0:T(8,128)S(1)} %get-tuple-element.18.block.refs_0_), channel_id=1, source_target_pairs={{0,3},{1,2},{2,1},{3,0},{4,7},{5,6},{6,5},{7,4},{8,11},{9,10},{10,... | collective-permute-start | bytes 98312 | tf_op jit(solution)/shard_map/ppermute | solution.py:436
  8.8 4.8 %collective-permute-start.1 = (f32[64,128]{1,0:T(8,128)S(1)}, f32[64,128]{1,0:T(8,128)S(1)}, u32[]{:S(2)}, u32[]{:S(2)}) collective-permute-start(f32[64,128]{1,0:T(8,128)S(1)} %get-tuple-element.18.block.refs_0_), channel_id=1, source_target_pairs={{0,2},{1,3},{2,0},{3,1},{4,6},{5,7},{6,4},{7,5},{8,10},{9,11},{10,... | collective-permute-start | bytes 98312 | tf_op jit(solution)/shard_map/ppermute | solution.py:436
  8.8 4.8 %collective-permute-start = (f32[64,128]{1,0:T(8,128)S(1)}, f32[64,128]{1,0:T(8,128)S(1)}, u32[]{:S(2)}, u32[]{:S(2)}) collective-permute-start(f32[64,128]{1,0:T(8,128)S(1)} %get-tuple-element.18.block.refs_0_), channel_id=1, source_target_pairs={{0,1},{1,0},{2,3},{3,2},{4,5},{5,4},{6,7},{7,6},{8,9},{9,8},{10,11... | collective-permute-start | bytes 98312 | tf_op jit(solution)/shard_map/ppermute | solution.py:436
  10.2 3.4 %collective-permute-start.4 = (f32[128,128]{1,0:T(8,128)S(1)}, f32[128,128]{1,0:T(8,128)S(1)}, u32[]{:S(2)}, u32[]{:S(2)}) collective-permute-start(f32[128,128]{1,0:T(8,128)S(1)} %join.1), channel_id=1, source_target_pairs={{0,4},{4,0},{8,12},{12,8},{1,5},{5,1},{9,13},{13,9},{2,6},{6,2},{1... | collective-permute-start | bytes 196616 | tf_op jit(solution)/shard_map/ppermute | solution.py:436
  17.5 5.6 %collective-permute-start.5 = (f32[128,128]{1,0:T(8,128)S(1)}, f32[128,128]{1,0:T(8,128)S(1)}, u32[]{:S(2)}, u32[]{:S(2)}) collective-permute-start(f32[128,128]{1,0:T(8,128)S(1)} %get-tuple-element.26), channel_id=1, source_target_pairs={{0,8},{4,12},{8,0},{12,4},{1,9},{5,13},{9,1},{13,5},{2,10},{6,14},... | collective-permute-start | bytes 196616 | tf_op jit(solution)/shard_map/ppermute | solution.py:436
  17.6 6.0 %collective-permute-start.6 = (f32[64,128]{1,0:T(8,128)S(1)}, f32[64,128]{1,0:T(8,128)S(1)}, u32[]{:S(2)}, u32[]{:S(2)}) collective-permute-start(f32[64,128]{1,0:T(8,128)S(1)} %get-tuple-element.28), channel_id=1, source_target_pairs={{0,3},{1,2},{2,1},{3,0},{4,7},{5,6},{6,5},{7,4},{8,11},{9,10},{10,... | collective-permute-start | bytes 98312 | tf_op jit(solution)/shard_map/ppermute | solution.py:436
  19.2 5.8 %collective-permute-start.7 = (f32[64,128]{1,0:T(8,128)S(1)}, f32[64,128]{1,0:T(8,128)S(1)}, u32[]{:S(2)}, u32[]{:S(2)}) collective-permute-start(f32[64,128]{1,0:T(8,128)S(1)} %get-tuple-element.29), channel_id=1, source_target_pairs={{0,2},{1,3},{2,0},{3,1},{4,6},{5,7},{6,4},{7,5},{8,10},{9,11},{10,... | collective-permute-start | bytes 98312 | tf_op jit(solution)/shard_map/ppermute | solution.py:436
  22.7 3.9 %collective-permute-start.8 = (f32[64,128]{1,0:T(8,128)S(1)}, f32[64,128]{1,0:T(8,128)S(1)}, u32[]{:S(2)}, u32[]{:S(2)}) collective-permute-start(f32[64,128]{1,0:T(8,128)S(1)} %get-tuple-element.30), channel_id=1, source_target_pairs={{0,1},{1,0},{2,3},{3,2},{4,5},{5,4},{6,7},{7,6},{8,9},{9,8},{10,11... | collective-permute-start | bytes 98312 | tf_op jit(solution)/shard_map/ppermute | solution.py:436
  23.2 3.4 %collective-permute-start.9 = (f32[64,128]{1,0:T(8,128)S(1)}, f32[64,128]{1,0:T(8,128)S(1)}, u32[]{:S(2)}, u32[]{:S(2)}) collective-permute-start(f32[64,128]{1,0:T(8,128)S(1)} %get-tuple-element.31), channel_id=1, source_target_pairs={{0,4},{4,0},{8,12},{12,8},{1,5},{5,1},{9,13},{13,9},{2,6},{6,2},{1... | collective-permute-start | bytes 98312 | tf_op jit(solution)/shard_map/ppermute | solution.py:436
